TPU v7x, 128 devices: a whole 4x4x4 slice. The times are simulated.
128 devices in a mesh: frame: 32 (over z, y_hi, x), head: 4 (over y_lo, core).
Axes of the slice: x: 4, y: 4 (y_hi: 2, y_lo: 2; y = y_hi * 2 + y_lo), z: 4, core: 2. Of those that a mesh axis runs over, the one named last changes fastest.
Arguments:
- queries: bfloat16 [24576, 3072], P('frame', 'head'), may hold values from -20 to 20
- keys: bfloat16 [24576, 3072], P('frame', 'head'), may hold values from -20 to 20
- values: bfloat16 [24576, 3072], P('frame', 'head'), may hold values from -6 to 6
- block_mask: int32 [192, 192], P('frame'), may hold values from 0 to 1, as said below
- out_weight: bfloat16 [3072, 3072], P('head'), may hold values from -0.4375 to 0.4375
Outputs:
- projected: bfloat16 [24576, 3072], P(('frame', 'head'))
Inputs may be any that keep to these rules, and one draw needn't show every extreme that they name: `block_mask`: group g holds the blocks g * 6 to (g + 1) * 6 - 1. A query block attends to every key block of its own group. Toward a group at distance d = 1, 2, 4 or 8 it attends to exactly max(1, 768 // (128 * 2 * d)) key blocks of that group, cyclically consecutive from a drawn start; to groups at any other distance to none.
All inputs are finite; a program needn't handle non-finite values.
Results may differ from a plain program's by a relative error of at most 0.015.
Values may be sent and summed in bfloat16 or wider, within the bound.
A program may use at most 320 MiB of HBM per device.

v0:
```python
import math

import jax
import jax.numpy as jnp
from jax import lax
from jax.experimental import pallas as pl
from jax.experimental.pallas import tpu as pltpu
from jax.sharding import PartitionSpec as P

HEAD_DIM = 128
BLK = 128
GROUP = 768
PER_GROUP = GROUP // BLK
WIDTH = 3072
HEADS_CHIP = 12
PLANE = 8
CHUNK = 512
CHUNKS = WIDTH // CHUNK
DISTANCES = (1, 2, 4, 8)
EXP2_SCALE = HEAD_DIM ** (-0.5) * math.log2(math.e)
NEG = -1e30
MESH = pl.DeviceIdType.MESH


def live_blocks(block_mask):
    me = lax.axis_index("frame")
    groups = lax.axis_size("frame")
    mask = block_mask.reshape(PER_GROUP, groups, PER_GROUP)
    begins = (mask > 0) & (jnp.roll(mask, 1, axis=2) == 0)
    first = jnp.sum(jnp.where(begins, jnp.arange(PER_GROUP, dtype=jnp.int32), 0), axis=2)
    offsets = jnp.array([s * d for d in DISTANCES for s in (-1, 1)], jnp.int32)
    wanted = jnp.arange(groups, dtype=jnp.int32)[:, None] == (me + offsets)[None, :]
    starts = jnp.sum(jnp.where(wanted[None], first[:, :, None], 0), axis=1)
    nearest = (starts[:, :2, None] + jnp.arange(3, dtype=jnp.int32)) % PER_GROUP
    blocks = jnp.concatenate([nearest.reshape(PER_GROUP, 6), starts[:, 2:]], axis=1)
    return jnp.zeros((8, 128), jnp.int32).at[:PER_GROUP, :12].set(blocks)


def kernel(
    q_hbm, k_hbm, v_hbm, blocks_ref, w_hbm, out_ref,
    plane, zbuf, qbuf, idx_v, idx_s, wbuf, acc, top_s, sum_s, obuf, att, sbuf, rbuf, own,
    kv_ss, q_ss, i_ss, pf_ss, z_ss, zf_ss, w_ss, o_ss, r_ss,
    p_rs, pf_rs, q_rs, i_rs, z_rs, zf_rs, w_rs, w_ls, a_rs, r_rs, s_sem,
):
    f = lax.axis_index("frame")
    h = lax.axis_index("head")
    z, yh, x = f // 8, lax.rem(f // 4, 2), lax.rem(f, 4)
    yl, c = h // 2, lax.rem(h, 2)
    g_me = lax.rem(f, 8)
    has_low, has_high = z > 0, z < 3

    def device(z_, g_, yl_, c_):
        return {"frame": z_ * 8 + g_, "head": yl_ * 2 + c_}

    other_core = device(z, g_me, yl, 1 - c)

    def remote(src, dst, ss, rs, target):
        return pltpu.make_async_remote_copy(
            src_ref=src, dst_ref=dst, send_sem=ss, recv_sem=rs, device_id=target, device_id_type=MESH
        )

    def is_me(target):
        return (target["frame"] == f) & (target["head"] == h)

    def send_or_copy(src, dst, ss, rs, target):
        mine = is_me(target)

        @pl.when(jnp.logical_not(mine))
        def _():
            remote(src, dst, ss, rs, target).start()

        @pl.when(mine)
        def _():
            pltpu.make_async_copy(src, dst, rs).start()

    def sent(src, dst, ss, rs, target):
        @pl.when(jnp.logical_not(is_me(target)))
        def _():
            remote(src, dst, ss, rs, target).wait_send()

    def arrived(ref, sem):
        pltpu.make_async_copy(ref, ref, sem).wait()

    barrier = pltpu.get_barrier_semaphore()

    def greet(target):
        pl.semaphore_signal(barrier, inc=1, device_id=target, device_id_type=MESH)

    def greet_plane(i, carry):
        target = device(z, i // 2, yl, lax.rem(i, 2))

        @pl.when(jnp.logical_not(is_me(target)))
        def _():
            greet(target)

        return carry

    lax.fori_loop(0, 2 * PLANE, greet_plane, 0)
    partner = [device(z, g_me, 1 - yl, c), device(z, (1 - yh) * 4 + x, 1 - yl, c)]
    for target in partner:
        greet(target)
    low, high = device(z - 1, g_me, yl, c), device(z + 1, g_me, yl, c)

    @pl.when(has_low)
    def _():
        greet(low)

    @pl.when(has_high)
    def _():
        greet(high)

    pl.semaphore_wait(barrier, 17 + has_low.astype(jnp.int32) + has_high.astype(jnp.int32))

    e_me = x + yh * (3 - 2 * x)

    def idx_copies():
        for i in range(2):
            for j in range(2):
                yield (blocks_ref, idx_v.at[e_me], i_ss.at[i, j], i_rs.at[e_me],
                       device(z, j * 4 + 2 * c + i, yl, yh))

    def kv_copies():
        for n, (j, to) in enumerate(((0, 0), (1, 1), (2, 0), (2, 1))):
            for i in range(2):
                for t, src in enumerate((k_hbm, v_hbm)):
                    hs = j // 2
                    yield (src.at[:, :, pl.ds((3 * i + j) * HEAD_DIM, HEAD_DIM)], plane.at[t, hs, g_me],
                           kv_ss.at[t, i, n], p_rs.at[hs, g_me], device(z, to * 4 + 2 * c + i, yl, t))

    def q_copies():
        for i in range(2):
            for j in range(3):
                to, slot = (j, e_me) if j < 2 else (e_me // 2, 4 + lax.rem(e_me, 2))
                yield (q_hbm.at[:, :, pl.ds((3 * i + j) * HEAD_DIM, HEAD_DIM)], qbuf.at[slot],
                       q_ss.at[i, j], q_rs.at[slot], device(z, to * 4 + 2 * c + i, yl, yh))

    for args in idx_copies():
        send_or_copy(*args)
    for args in kv_copies():
        send_or_copy(*args)
    for args in q_copies():
        send_or_copy(*args)
    w_local = pltpu.make_async_copy(w_hbm, wbuf.at[c], w_ls)
    w_remote = remote(w_hbm, wbuf.at[c], w_ss, w_rs, other_core)
    w_local.start()

    def piece(step):
        hs = step // PLANE
        g = lax.bitwise_xor(lax.rem(step, PLANE), g_me)
        return hs, g

    def to_high(hs, g):
        return (hs == 0) | (g // 2 != 1 - yh)

    def to_low(hs, g):
        return (hs == 0) | (g // 2 != 2 + yh)

    def z_copy(way, hs, g):
        return remote(plane.at[c, hs, g], zbuf.at[way, c, hs, g], z_ss.at[way, hs, g], z_rs.at[way, hs, g],
                      (high, low)[way])

    def plane_forward(hs, g):
        return remote(plane.at[c, hs, g], plane.at[c, hs, g], pf_ss.at[hs, g], pf_rs.at[hs, g], other_core)

    def z_forward(way, hs, g):
        return remote(zbuf.at[way, c, hs, g], zbuf.at[way, c, hs, g], zf_ss.at[way, hs, g], zf_rs.at[way, hs, g],
                      other_core)

    def spread(step, carry):
        hs, g = piece(step)
        arrived(plane.at[c, hs, g], p_rs.at[hs, g])

        @pl.when(has_high & to_high(hs, g))
        def _():
            z_copy(0, hs, g).start()

        @pl.when(has_low & to_low(hs, g))
        def _():
            z_copy(1, hs, g).start()

        plane_forward(hs, g).start()
        return carry

    def gets(way, hs, g):
        return (has_low & to_high(hs, g), has_high & to_low(hs, g))[way]

    def pass_on(step, carry):
        hs, g = piece(step)
        for way in range(2):

            @pl.when(gets(way, hs, g))
            def _():
                arrived(zbuf.at[way, c, hs, g], z_rs.at[way, hs, g])
                z_forward(way, hs, g).start()

        return carry

    lax.fori_loop(0, 2 * PLANE, spread, 0)
    w_remote.start()
    lax.fori_loop(0, 8, pass_on, 0)

    def other_plane(step, carry):
        hs, g = piece(step)
        arrived(plane.at[1 - c, hs, g], pf_rs.at[hs, g])
        return carry

    lax.fori_loop(0, 2 * PLANE, other_plane, 0)
    for e in range(4):
        arrived(idx_v.at[e], i_rs.at[e])
    load_idx = pltpu.make_async_copy(idx_v, idx_s, s_sem)
    load_idx.start()
    load_idx.wait()
    for u in range(6):
        arrived(qbuf.at[u], q_rs.at[u])

    def frame_at(e):
        return e + c * (7 - 2 * e)

    def scores_of(q, keys):
        return lax.dot_general(q, keys, (((1,), (1,)), ((), ())), preferred_element_type=jnp.float32)

    def rows_at(qb):
        return pl.ds(pl.multiple_of(qb * BLK, BLK), BLK)

    def block(e, qb, d, way, j=0):
        return idx_s[e, qb, 3 * way + j if d == 0 else 4 + 2 * d + way]

    def plane_part(u, e, hs, out1, out2, qb):
        g = frame_at(e)
        near = [(frame_at(e + 1), block(e, qb, 0, 1 - c, j)) for j in range(3)]
        near += [(frame_at(e + 2), block(e, qb, 1, 1 - c)), (frame_at(e + 4), block(e, qb, 2, 1 - c))]
        if out1:
            near += [(frame_at(e - 1), block(e, qb, 0, c, j)) for j in range(3)]
        if out2:
            near += [(frame_at(e - 2), block(e, qb, 1, c))]
        q = qbuf[u, qb]

        def taken(t):
            return jnp.concatenate(
                [plane[t, hs, g].reshape(GROUP, HEAD_DIM)] + [plane[t, hs, gg, b] for gg, b in near], axis=0
            )

        keys, vals = taken(0), taken(1)
        s = scores_of(q, keys)
        top = jnp.max(s, axis=1, keepdims=True)
        p = jnp.exp2((s - top) * EXP2_SCALE)
        total = jnp.sum(p, axis=1, keepdims=True)
        acc[u, rows_at(qb), :] = jnp.dot(p.astype(jnp.bfloat16), vals, preferred_element_type=jnp.float32)
        top_s[u, rows_at(qb), :] = jnp.broadcast_to(top, (BLK, HEAD_DIM))
        sum_s[u, rows_at(qb), :] = jnp.broadcast_to(total, (BLK, HEAD_DIM))

    def z_part(u, e, hs, out1, out2, qb):
        g = frame_at(e)
        far = [(0, g, block(e, qb, 3, 0)), (1, g, block(e, qb, 3, 1)), (c, frame_at(e + 4), block(e, qb, 2, c))]
        if not out2:
            far += [(c, frame_at(e + 6), block(e, qb, 1, c))]
        if not out1:
            far += [(c, frame_at(e + 7), block(e, qb, 0, c, j)) for j in range(3)]
        q = qbuf[u, qb]
        keys, vals, valid = [], [], []
        for way, gg, b in far:
            ok = ((way == 0) & has_low) | ((way == 1) & has_high)
            w2 = jnp.where(ok, way, 1 - way)
            g2 = jnp.where(ok, gg, g)
            keys.append(zbuf[w2, 0, hs, g2, b])
            vals.append(zbuf[w2, 1, hs, g2, b])
            valid.append(jnp.where(ok, 0.0, NEG))
        s = scores_of(q, jnp.concatenate(keys, axis=0))
        s = jnp.concatenate(
            [s[:, n * BLK : (n + 1) * BLK] + valid[n] for n in range(len(far))], axis=1
        )
        old = top_s[u, rows_at(qb), :]
        top = jnp.maximum(old[:, :1], jnp.max(s, axis=1, keepdims=True))
        p = jnp.exp2((s - top) * EXP2_SCALE)
        keep = jnp.exp2((old - top) * EXP2_SCALE)
        total = sum_s[u, rows_at(qb), :] * keep + jnp.sum(p, axis=1, keepdims=True)
        o = acc[u, rows_at(qb), :] * keep + jnp.dot(
            p.astype(jnp.bfloat16), jnp.concatenate(vals, axis=0), preferred_element_type=jnp.float32
        )
        obuf[u, rows_at(qb), :] = (o / total).astype(jnp.bfloat16)

    kinds = (
        (2 - yh, lambda n: (4 * n, 0, n), False, False),
        (2 - yh, lambda n: (1 + 4 * n, 1, n), True, False),
        (2 + 2 * yh, lambda n: (2 + n, 2 + lax.rem(n, 2), n // 2), True, True),
    )
    for step, (count, unit, out1, out2) in enumerate(kinds):

        def plane_unit(n, carry, unit=unit, out1=out1, out2=out2):
            u, e, hs = unit(n)

            def one(qb, carry2):
                plane_part(u, e, hs, out1, out2, qb)
                return carry2

            return lax.fori_loop(0, PER_GROUP, one, carry)

        lax.fori_loop(0, count, plane_unit, 0)
        lax.fori_loop(8 + 2 * step, 10 + 2 * step, pass_on, 0)
    lax.fori_loop(14, 16, pass_on, 0)

    def other_z(step, carry):
        hs, g = piece(step)
        for way in range(2):

            @pl.when(gets(way, hs, g))
            def _():
                arrived(zbuf.at[way, 1 - c, hs, g], zf_rs.at[way, hs, g])

        return carry

    lax.fori_loop(0, 2 * PLANE, other_z, 0)

    def o_copies(u, e, hs):
        head = 3 * x + jnp.where(hs == 0, yh, 2)
        cols = pl.ds(pl.multiple_of(head * HEAD_DIM, HEAD_DIM), HEAD_DIM)
        x_to = e + c * (3 - 2 * e)
        here, across = c * 4 + x_to, (1 - c) * 4 + x_to
        for t in range(2):
            mine, theirs = (2 * yl + t) * 192, (2 * (1 - yl) + t) * 192
            parts = ((mine, 192, 192, here), (theirs, 96, 0, here), (theirs + 96, 96, 96, across))
            for k, (row, size, at, to) in enumerate(parts):
                yield (obuf.at[u, pl.ds(pl.multiple_of(row, 96), size), :], att.at[pl.ds(at, size), cols],
                       o_ss.at[u, t, k], a_rs.at[k], device(z, to, yl, t))

    for count, unit, out1, out2 in kinds:

        def z_unit(n, carry, unit=unit, out1=out1, out2=out2):
            u, e, hs = unit(n)

            def one(qb, carry2):
                z_part(u, e, hs, out1, out2, qb)
                return carry2

            lax.fori_loop(0, PER_GROUP, one, 0)
            for args in o_copies(u, e, hs):
                send_or_copy(*args)
            return carry

        lax.fori_loop(0, count, z_unit, 0)

    w_local.wait()
    arrived(wbuf.at[1 - c], w_rs)
    arrived(att.at[pl.ds(192, 192)], a_rs.at[0])
    arrived(att.at[pl.ds(0, 96)], a_rs.at[1])
    arrived(att.at[pl.ds(96, 96)], a_rs.at[2])

    def r_copy(n, k):
        cols = pl.ds(pl.multiple_of(n * CHUNK, CHUNK), CHUNK)
        rows = pl.ds(96 * k, 96)
        return remote(sbuf.at[rows, cols], rbuf.at[rows, cols], r_ss.at[n, k], r_rs.at[n, k], partner[k])

    half = HEADS_CHIP // 2 * HEAD_DIM

    def project(n, carry):
        cols = pl.ds(pl.multiple_of(n * CHUNK, CHUNK), CHUNK)
        r = jnp.dot(att[:, :half], wbuf[0, :, cols], preferred_element_type=jnp.float32)
        r = r + jnp.dot(att[:, half:], wbuf[1, :, cols], preferred_element_type=jnp.float32)
        sbuf[:, cols] = r[:192].astype(jnp.bfloat16)
        own[:, cols] = r[192:]
        for k in range(2):
            r_copy(n, k).start()
        return carry

    lax.fori_loop(0, CHUNKS, project, 0)

    def finish(n, carry):
        cols = pl.ds(pl.multiple_of(n * CHUNK, CHUNK), CHUNK)
        for k in range(2):
            r_copy(n, k).wait()
        out_ref[:, cols] = (own[:, cols] + rbuf[:, cols].astype(jnp.float32)).astype(jnp.bfloat16)
        return carry

    lax.fori_loop(0, CHUNKS, finish, 0)

    for copies in (idx_copies, kv_copies, q_copies):
        for args in copies():
            sent(*args)
    w_remote.wait_send()

    def done(step, carry):
        hs, g = piece(step)
        plane_forward(hs, g).wait_send()

        @pl.when(has_high & to_high(hs, g))
        def _():
            z_copy(0, hs, g).wait_send()

        @pl.when(has_low & to_low(hs, g))
        def _():
            z_copy(1, hs, g).wait_send()

        for way in range(2):

            @pl.when(gets(way, hs, g))
            def _():
                z_forward(way, hs, g).wait_send()

        return carry

    lax.fori_loop(0, 2 * PLANE, done, 0)
    for count, unit, out1, out2 in kinds:

        def o_done(n, carry, unit=unit):
            for args in o_copies(*unit(n)):
                sent(*args)
            return carry

        lax.fori_loop(0, count, o_done, 0)


def per_device(queries, keys, values, block_mask, out_weight):
    blocks = live_blocks(block_mask)
    dma = pltpu.SemaphoreType.DMA
    bf16, f32 = jnp.bfloat16, jnp.float32
    rows, piece = (GROUP, HEAD_DIM), (PER_GROUP, BLK, HEAD_DIM)
    scratch = [
        pltpu.VMEM((2, 2, PLANE, *piece), bf16),
        pltpu.VMEM((2, 2, 2, PLANE, *piece), bf16),
        pltpu.VMEM((6, *piece), bf16),
        pltpu.VMEM((4, 8, 128), jnp.int32),
        pltpu.SMEM((4, 8, 128), jnp.int32),
        pltpu.VMEM((2, *out_weight.shape), bf16),
        pltpu.VMEM((6, *rows), f32),
        pltpu.VMEM((6, *rows), f32),
        pltpu.VMEM((6, *rows), f32),
        pltpu.VMEM((6, *rows), bf16),
        pltpu.VMEM((384, HEADS_CHIP * HEAD_DIM), bf16),
        pltpu.VMEM((192, WIDTH), bf16),
        pltpu.VMEM((192, WIDTH), bf16),
        pltpu.VMEM((192, WIDTH), f32),
        dma((2, 2, 4)), dma((2, 3)), dma((2, 2)), dma((2, 8)), dma((2, 2, 8)), dma((2, 2, 8)), dma, dma((6, 2, 3)),
        dma((CHUNKS, 2)),
        dma((2, 8)), dma((2, 8)), dma((6,)), dma((4,)), dma((2, 2, 8)), dma((2, 2, 8)), dma, dma, dma((3,)),
        dma((CHUNKS, 2)), dma,
    ]
    any_space = pl.BlockSpec(memory_space=pl.ANY)
    vmem = pl.BlockSpec(memory_space=pltpu.VMEM)
    return pl.pallas_call(
        kernel,
        out_shape=jax.ShapeDtypeStruct((192, WIDTH), bf16),
        in_specs=[any_space, any_space, any_space, vmem, any_space],
        out_specs=vmem,
        scratch_shapes=scratch,
        compiler_params=pltpu.CompilerParams(
            collective_id=0, has_side_effects=True, vmem_limit_bytes=60 * 2**20
        ),
        name="attention",
    )(*(a.reshape(PER_GROUP, BLK, GROUP) for a in (queries, keys, values)), blocks, out_weight)


def solution(mesh):
    in_specs = (
        P("frame", "head"),
        P("frame", "head"),
        P("frame", "head"),
        P("frame", None),
        P("head", None),
    )
    out_specs = P(("frame", "head"), None)
    return jax.shard_map(
        per_device, mesh=mesh, in_specs=in_specs, out_specs=out_specs, check_vma=False
    )
```

profile of v0, /device:TPU:39, one launch (start us, length us, event | category | flops | bytes accessed | tf_op | source)
XLA Modules:
  0.0 145.1 jit_solution(312092133324569951)
XLA Ops:
  0.0 0.7 broadcast_add_fusion
  0.7 0.1 iota_compare_fusion
  0.7 0.1 add.42
  0.8 0.8 reshape.72
  1.6 0.1 slice.38
  1.7 0.3 select_reduce_fusion
  2.0 0.2 select_reduce_fusion.1
  2.2 0.1 copy.16
  2.3 0.1 copy.17
  2.4 0.1 slice.37
  2.5 0.1 pad_add_fusion
  2.6 0.6 scatter.4.blocks_ref
  3.2 139.5 %attention.1 = bf16[192,3072]{1,0:T(8,128)(2,1)} custom-call(bf16[6,128,768]{2,1,0:T(8,128)(2,1)} %bitcast.8, bf16[6,128,768]{2,1,0:T(8,128)(2,1)} %bitcast.9, bf16[6,128,768]{2,1,0:T(8,128)(2,1)} %bitcast.10, s32[8,128]{1,0:T(8,128)} %scatter.4.blocks_ref, bf16[768,3072]{1,0:T(8,128)(2,1)} %w_hbm.1), custom_call_target="tpu_custom_call" | custom-call | tf_op jit(solution)/shard_map/attention/pallas_call | solution.py:439
  142.7 2.4 %copy.19 = bf16[192,3072]{1,0:T(8,128)(2,1)} copy(bf16[192,3072]{1,0:T(8,128)(2,1)} %attention.1) | data formatting | bytes 2359296
  (4 shorter events, 0.0 us)
where the time goes:
time: 145 us
  Pallas kernels  140 us (97%)
  local copies, waits for them, and re-layouts  4.22 us (3%)
    pallas_call x1, Pallas kernels, per_device(): pl.pallas_call(kernel, out_shape=jax.ShapeDtypeStruct((192, WIDTH), bf16)...  140 us

commit v1 on v0

v1 whole, which is shorter than its diff:
```python
import math

import jax
import jax.numpy as jnp
from jax import lax
from jax.experimental import pallas as pl
from jax.experimental.pallas import tpu as pltpu
from jax.sharding import PartitionSpec as P

HEAD_DIM = 128
BLK = 128
GROUP = 768
PER_GROUP = GROUP // BLK
WIDTH = 3072
HEADS_CHIP = 12
PLANE = 8
CHUNK = 512
CHUNKS = WIDTH // CHUNK
EXP2_SCALE = HEAD_DIM ** (-0.5) * math.log2(math.e)
NEG = -1e30
MESH = pl.DeviceIdType.MESH


def live_blocks(mask):
    lane = lax.broadcasted_iota(jnp.int32, mask.shape, 1)
    at = lax.rem(lane, PER_GROUP)
    lanes = mask.shape[1]

    def ahead(value, by):
        return pltpu.roll(value, (lanes - by) % lanes, 1)

    before = jnp.where(at == 0, ahead(mask, PER_GROUP - 1), ahead(mask, lanes - 1))
    first = jnp.where((mask > 0) & (before == 0), at, 0)
    total = first
    for n in range(1, PER_GROUP):
        total = total + ahead(first, n)
    total = jnp.where((at == 0) & (lane < lanes - PER_GROUP), total, 0)
    shared = total
    for n in range(1, PER_GROUP):
        shared = shared + ahead(total, lanes - n)
    return lax.rem(shared + at, PER_GROUP)


def kernel(
    q_hbm, k_hbm, v_hbm, mask_ref, w_hbm, out_ref,
    plane_a, plane_c, z_a, z_c, qbuf, blocks_ref, idx_v, idx_s, w_a, w_c, acc, top_s, sum_s, obuf, att_a, att_c,
    sums, sbuf, rbuf,
    kv_ss, q_ss, i_ss, pf_ss, z_ss, zf_ss, w_ss, o_ss, r_ss,
    p_rs, pf_rs, q_rs, i_rs, z_rs, zf_rs, w_rs, w_ls, a_rs, r_rs, s_sem,
):
    plane, zbuf, att, wbuf = (plane_a, plane_c), (z_a, z_c), (att_a, att_c), (w_a, w_c)
    f = lax.axis_index("frame")
    h = lax.axis_index("head")
    z, yh, x = f // 8, lax.rem(f // 4, 2), lax.rem(f, 4)
    yl, c = h // 2, lax.rem(h, 2)
    g_me = lax.rem(f, 8)
    has_low, has_high = z > 0, z < 3

    def device(z_, g_, yl_, c_):
        return {"frame": z_ * 8 + g_, "head": yl_ * 2 + c_}

    other_core = device(z, g_me, yl, 1 - c)

    def remote(src, dst, ss, rs, target):
        return pltpu.make_async_remote_copy(
            src_ref=src, dst_ref=dst, send_sem=ss, recv_sem=rs, device_id=target, device_id_type=MESH
        )

    def is_me(target):
        return (target["frame"] == f) & (target["head"] == h)

    def send_or_copy(src, dst, ss, rs, target):
        mine = is_me(target)

        @pl.when(jnp.logical_not(mine))
        def _():
            remote(src, dst, ss, rs, target).start()

        @pl.when(mine)
        def _():
            pltpu.make_async_copy(src, dst, rs).start()

    def sent(src, dst, ss, rs, target):
        @pl.when(jnp.logical_not(is_me(target)))
        def _():
            remote(src, dst, ss, rs, target).wait_send()

    def arrived(ref, sem):
        pltpu.make_async_copy(ref, ref, sem).wait()

    barrier = pltpu.get_barrier_semaphore()

    def greet(target):
        pl.semaphore_signal(barrier, inc=1, device_id=target, device_id_type=MESH)

    def greet_plane(i, carry):
        target = device(z, i // 2, yl, lax.rem(i, 2))

        @pl.when(jnp.logical_not(is_me(target)))
        def _():
            greet(target)

        return carry

    lax.fori_loop(0, 2 * PLANE, greet_plane, 0)
    partner = [device(z, g_me, 1 - yl, c), device(z, (1 - yh) * 4 + x, 1 - yl, c)]
    for target in partner:
        greet(target)
    low, high = device(z - 1, g_me, yl, c), device(z + 1, g_me, yl, c)

    @pl.when(has_low)
    def _():
        greet(low)

    @pl.when(has_high)
    def _():
        greet(high)

    blocks_ref[...] = jnp.zeros_like(blocks_ref)
    blocks_ref[:PER_GROUP, : mask_ref.shape[1]] = mask_ref[...]
    blocks_ref[...] = live_blocks(blocks_ref[...])
    pl.semaphore_wait(barrier, 17 + has_low.astype(jnp.int32) + has_high.astype(jnp.int32))

    e_me = x + yh * (3 - 2 * x)

    def idx_copies():
        for i in range(2):
            for j in range(2):
                yield (blocks_ref, idx_v.at[e_me], i_ss.at[i, j], i_rs.at[e_me],
                       device(z, j * 4 + 2 * c + i, yl, yh))

    def kv_copies(hs):
        for n, (j, to) in (((0, (0, 0)), (1, (1, 1))), ((2, (2, 0)), (3, (2, 1))))[hs]:
            for i in range(2):
                for t, src in enumerate((k_hbm, v_hbm)):
                    yield (src.at[:, :, pl.ds((3 * i + j) * HEAD_DIM, HEAD_DIM)], plane[hs].at[t, g_me],
                           kv_ss.at[t, i, n], p_rs.at[hs, g_me], device(z, to * 4 + 2 * c + i, yl, t))

    def q_copies(hs):
        for i in range(2):
            for j in ((0, 1), (2,))[hs]:
                to, slot = (j, e_me) if j < 2 else (e_me // 2, 4 + lax.rem(e_me, 2))
                yield (q_hbm.at[:, :, pl.ds((3 * i + j) * HEAD_DIM, HEAD_DIM)], qbuf.at[slot],
                       q_ss.at[i, j], q_rs.at[slot], device(z, to * 4 + 2 * c + i, yl, yh))

    dealt = (lambda: kv_copies(0), idx_copies, lambda: q_copies(0), lambda: kv_copies(1), lambda: q_copies(1))
    for copies in dealt:
        for args in copies():
            send_or_copy(*args)

    def w_copies():
        for i in range(2):
            for hs, size in enumerate((256, 128)):
                yield (w_hbm.at[pl.ds(384 * i + 256 * hs, size), :],
                       wbuf[hs].at[pl.ds(pl.multiple_of((2 * c + i) * size, size), size), :], i, hs)

    for src, dst, i, hs in w_copies():
        pltpu.make_async_copy(src, dst, w_ls.at[i, hs]).start()

    def frame_of(step):
        return lax.bitwise_xor(step, g_me)

    def to_high(hs, g):
        return (g // 2 != 1 - yh) if hs else (g >= 0)

    def to_low(hs, g):
        return (g // 2 != 2 + yh) if hs else (g >= 0)

    def z_copy(way, hs, g):
        return remote(plane[hs].at[c, g], zbuf[hs].at[way, c, g], z_ss.at[way, hs, g], z_rs.at[way, hs, g],
                      (high, low)[way])

    def plane_forward(hs, g):
        return remote(plane[hs].at[c, g], plane[hs].at[c, g], pf_ss.at[hs, g], pf_rs.at[hs, g], other_core)

    def z_forward(way, hs, g):
        return remote(zbuf[hs].at[way, c, g], zbuf[hs].at[way, c, g], zf_ss.at[way, hs, g], zf_rs.at[way, hs, g],
                      other_core)

    def spread(hs, first, last):
        def one(step, carry):
            g = frame_of(step)
            arrived(plane[hs].at[c, g], p_rs.at[hs, g])

            @pl.when(has_high & to_high(hs, g))
            def _():
                z_copy(0, hs, g).start()

            @pl.when(has_low & to_low(hs, g))
            def _():
                z_copy(1, hs, g).start()

            plane_forward(hs, g).start()
            return carry

        lax.fori_loop(first, last, one, 0)

    def gets(way, hs, g):
        return (has_low & to_high(hs, g), has_high & to_low(hs, g))[way]

    def pass_on(hs, first, last):
        def one(step, carry):
            g = frame_of(step)
            for way in range(2):

                @pl.when(gets(way, hs, g))
                def _():
                    arrived(zbuf[hs].at[way, c, g], z_rs.at[way, hs, g])
                    z_forward(way, hs, g).start()

            return carry

        lax.fori_loop(first, last, one, 0)

    def other_plane(hs):
        def one(g, carry):
            arrived(plane[hs].at[1 - c, g], pf_rs.at[hs, g])
            return carry

        lax.fori_loop(0, PLANE, one, 0)

    def other_z(hs):
        def one(g, carry):
            for way in range(2):

                @pl.when(gets(way, hs, g))
                def _():
                    arrived(zbuf[hs].at[way, 1 - c, g], zf_rs.at[way, hs, g])

            return carry

        lax.fori_loop(0, PLANE, one, 0)

    def frame_at(e):
        return e + c * (7 - 2 * e)

    def scores_of(q, keys):
        return lax.dot_general(q, keys, (((1,), (1,)), ((), ())), preferred_element_type=jnp.float32)

    def rows_at(qb):
        return pl.ds(pl.multiple_of(qb * BLK, BLK), BLK)

    def block(e, qb, distance, way, j=0):
        group = z * PLANE + frame_at(e) + (2 * way - 1) * distance
        group = jnp.clip(group, 0, 4 * PLANE - 1)
        return idx_s[e, qb, group * PER_GROUP + j]

    def plane_part(u, e, hs, out1, out2, qb):
        g = frame_at(e)
        near = [(frame_at(e + 1), block(e, qb, 1, 1 - c, j)) for j in range(3)]
        near += [(frame_at(e + 2), block(e, qb, 2, 1 - c)), (frame_at(e + 4), block(e, qb, 4, 1 - c))]
        if out1:
            near += [(frame_at(e - 1), block(e, qb, 1, c, j)) for j in range(3)]
        if out2:
            near += [(frame_at(e - 2), block(e, qb, 2, c))]
        q = qbuf[u, qb]

        def taken(t):
            return jnp.concatenate(
                [plane[hs][t, g].reshape(GROUP, HEAD_DIM)] + [plane[hs][t, gg, b] for gg, b in near], axis=0
            )

        keys, vals = taken(0), taken(1)
        s = scores_of(q, keys)
        top = jnp.max(s, axis=1, keepdims=True)
        p = jnp.exp2((s - top) * EXP2_SCALE)
        total = jnp.sum(p, axis=1, keepdims=True)
        acc[u, rows_at(qb), :] = jnp.dot(p.astype(jnp.bfloat16), vals, preferred_element_type=jnp.float32)
        top_s[u, rows_at(qb), :] = jnp.broadcast_to(top, (BLK, HEAD_DIM))
        sum_s[u, rows_at(qb), :] = jnp.broadcast_to(total, (BLK, HEAD_DIM))

    def z_part(u, e, hs, out1, out2, qb):
        g = frame_at(e)
        far = [(0, g, block(e, qb, 8, 0)), (1, g, block(e, qb, 8, 1)), (c, frame_at(e + 4), block(e, qb, 4, c))]
        if not out2:
            far += [(c, frame_at(e + 6), block(e, qb, 2, c))]
        if not out1:
            far += [(c, frame_at(e + 7), block(e, qb, 1, c, j)) for j in range(3)]
        q = qbuf[u, qb]
        keys, vals, valid = [], [], []
        for way, gg, b in far:
            ok = ((way == 0) & has_low) | ((way == 1) & has_high)
            w2 = jnp.where(ok, way, 1 - way)
            g2 = jnp.where(ok, gg, g)
            keys.append(zbuf[hs][w2, 0, g2, b])
            vals.append(zbuf[hs][w2, 1, g2, b])
            valid.append(jnp.where(ok, 0.0, NEG))
        s = scores_of(q, jnp.concatenate(keys, axis=0))
        s = jnp.concatenate(
            [s[:, n * BLK : (n + 1) * BLK] + valid[n] for n in range(len(far))], axis=1
        )
        old = top_s[u, rows_at(qb), :]
        top = jnp.maximum(old[:, :1], jnp.max(s, axis=1, keepdims=True))
        p = jnp.exp2((s - top) * EXP2_SCALE)
        keep = jnp.exp2((old - top) * EXP2_SCALE)
        total = sum_s[u, rows_at(qb), :] * keep + jnp.sum(p, axis=1, keepdims=True)
        o = acc[u, rows_at(qb), :] * keep + jnp.dot(
            p.astype(jnp.bfloat16), jnp.concatenate(vals, axis=0), preferred_element_type=jnp.float32
        )
        obuf[u, rows_at(qb), :] = (o / total).astype(jnp.bfloat16)

    def query_blocks(first, last, unroll, part, *unit):
        def one(qb, carry):
            part(*unit, first + qb)
            return carry

        lax.fori_loop(0, last, one, 0, unroll=unroll)

    def o_copies(u, e, hs, ks):
        head = x if hs else 2 * x + yh
        cols = pl.ds(pl.multiple_of(head * HEAD_DIM, HEAD_DIM), HEAD_DIM)
        x_to = e + c * (3 - 2 * e)
        here, across = c * 4 + x_to, (1 - c) * 4 + x_to
        for t in range(2):
            mine, theirs = (2 * yl + t) * 192, (2 * (1 - yl) + t) * 192
            parts = ((mine, 192, 192, here), (theirs, 96, 0, here), (theirs + 96, 96, 96, across))
            for k in ks:
                row, size, at, to = parts[k]
                yield (obuf.at[u, pl.ds(pl.multiple_of(row, 96), size), :], att[hs].at[pl.ds(at, size), cols],
                       o_ss.at[u, t, k], a_rs.at[hs, k], device(z, to, yl, t))

    def att_arrived(hs, ks):
        for k in ks:
            row, size = ((192, 192), (0, 96), (96, 96))[k]
            arrived(att[hs].at[pl.ds(row, size)], a_rs.at[hs, k])

    own_kinds = (
        (1, lambda n: (0, 0), False, False),
        (1, lambda n: (1, 1), True, False),
        (2, lambda n: (2 + n, 2 + n), True, True),
    )
    shared_kinds = (
        (1 - yh, lambda n: (4, 0), False, False),
        (1 - yh, lambda n: (5, 1), True, False),
        (2 * yh, lambda n: (4 + n, 2 + n), True, True),
    )

    spread(0, 0, PLANE)
    for src, dst, i, hs in w_copies():
        remote(src, dst, w_ss.at[i, hs], w_rs.at[i, hs], other_core).start()
    for e in range(4):
        arrived(idx_v.at[e], i_rs.at[e])
    load_idx = pltpu.make_async_copy(idx_v, idx_s, s_sem)
    load_idx.start()
    other_plane(0)
    load_idx.wait()
    for u in range(4):
        arrived(qbuf.at[u], q_rs.at[u])
    for count, unit, out1, out2 in own_kinds:

        def own_plane(n, carry, unit=unit, out1=out1, out2=out2):
            u, e = unit(n)
            query_blocks(0, PER_GROUP, 3, plane_part, u, e, 0, out1, out2)
            spread(1, 2 * u, 2 * u + 2)
            pass_on(0, 2 * u, 2 * u + 2)
            return carry

        lax.fori_loop(0, count, own_plane, 0)
    other_z(0)
    for count, unit, out1, out2 in own_kinds:

        def own_far(n, carry, unit=unit, out1=out1, out2=out2):
            u, e = unit(n)
            query_blocks(0, PER_GROUP, 6, z_part, u, e, 0, out1, out2)
            for args in o_copies(u, e, 0, range(3)):
                send_or_copy(*args)
            return carry

        lax.fori_loop(0, count, own_far, 0)
    pass_on(1, 0, 1)
    other_plane(1)
    for u in range(4, 6):
        arrived(qbuf.at[u], q_rs.at[u])
    for count, unit, out1, out2 in shared_kinds:

        def shared_plane(n, carry, unit=unit, out1=out1, out2=out2):
            u, e = unit(n)
            query_blocks(0, PER_GROUP, 3, plane_part, u, e, 1, out1, out2)
            pass_on(1, u - 3, u - 2)
            return carry

        lax.fori_loop(0, count, shared_plane, 0)

    for src, dst, i, hs in w_copies():
        pltpu.make_async_copy(src, dst, w_ls.at[i, hs]).wait()
    for i in range(2):
        for hs, size in enumerate((256, 128)):
            arrived(wbuf[hs].at[pl.ds(pl.multiple_of((2 * (1 - c) + i) * size, size), size), :], w_rs.at[i, hs])
    att_arrived(0, range(3))

    def cols_at(n):
        return pl.ds(pl.multiple_of(n * CHUNK, CHUNK), CHUNK)

    def project_own(n, carry):
        sums[:, cols_at(n)] = jnp.dot(att_a[...], w_a[:, cols_at(n)], preferred_element_type=jnp.float32)
        return carry

    def project_and_pass(n, carry):
        project_own(n, carry)
        pass_on(1, n + 3, n + 4)
        return carry

    lax.fori_loop(0, 5, project_and_pass, 0)
    lax.fori_loop(5, CHUNKS, project_own, 0)
    other_z(1)
    for ks, first in (((1, 2), 3 * (1 - yl)), ((0,), 3 * yl)):
        for count, unit, out1, out2 in shared_kinds:

            def shared_far(n, carry, unit=unit, out1=out1, out2=out2):
                u, e = unit(n)
                query_blocks(first, 3, 3, z_part, u, e, 1, out1, out2)
                for args in o_copies(u, e, 1, ks):
                    send_or_copy(*args)
                return carry

            lax.fori_loop(0, count, shared_far, 0)

    def r_copy(n, k):
        rows = pl.ds(96 * k, 96)
        return remote(sbuf.at[rows, cols_at(n)], rbuf.at[rows, cols_at(n)], r_ss.at[n, k], r_rs.at[n, k], partner[k])

    def project_theirs(n, carry):
        r = jnp.dot(att_c[:192], w_c[:, cols_at(n)], preferred_element_type=jnp.float32)
        sbuf[:, cols_at(n)] = (r + sums[:192, cols_at(n)]).astype(jnp.bfloat16)
        for k in range(2):
            r_copy(n, k).start()
        return carry

    def project_mine(n, carry):
        r = jnp.dot(att_c[192:], w_c[:, cols_at(n)], preferred_element_type=jnp.float32)
        sums[192:, cols_at(n)] = r + sums[192:, cols_at(n)]
        return carry

    def finish(n, carry):
        for k in range(2):
            r_copy(n, k).wait()
        total = sums[192:, cols_at(n)] + rbuf[:, cols_at(n)].astype(jnp.float32)
        out_ref[:, cols_at(n)] = total.astype(jnp.bfloat16)
        return carry

    att_arrived(1, (1, 2))
    lax.fori_loop(0, CHUNKS, project_theirs, 0)
    att_arrived(1, (0,))
    lax.fori_loop(0, CHUNKS, project_mine, 0)
    lax.fori_loop(0, CHUNKS, finish, 0)

    for copies in dealt:
        for args in copies():
            sent(*args)
    for src, dst, i, hs in w_copies():
        remote(src, dst, w_ss.at[i, hs], w_rs.at[i, hs], other_core).wait_send()

    def done(g, carry):
        for hs in range(2):
            plane_forward(hs, g).wait_send()

            @pl.when(has_high & to_high(hs, g))
            def _():
                z_copy(0, hs, g).wait_send()

            @pl.when(has_low & to_low(hs, g))
            def _():
                z_copy(1, hs, g).wait_send()

            for way in range(2):

                @pl.when(gets(way, hs, g))
                def _():
                    z_forward(way, hs, g).wait_send()

        return carry

    lax.fori_loop(0, PLANE, done, 0)

    def o_done(u, e, hs):
        for args in o_copies(u, e, hs, range(3)):
            sent(*args)

    def own_done(n, carry):
        o_done(n, n, 0)
        return carry

    def shared_done(n, carry):
        o_done(4 + n, 2 * yh + n, 1)
        return carry

    lax.fori_loop(0, 4, own_done, 0)
    lax.fori_loop(0, 2, shared_done, 0)


def per_device(queries, keys, values, block_mask, out_weight):
    dma = pltpu.SemaphoreType.DMA
    bf16, f32 = jnp.bfloat16, jnp.float32
    rows, piece = (GROUP, HEAD_DIM), (PER_GROUP, BLK, HEAD_DIM)
    scratch = [
        pltpu.VMEM((2, PLANE, *piece), bf16), pltpu.VMEM((2, PLANE, *piece), bf16),
        pltpu.VMEM((2, 2, PLANE, *piece), bf16), pltpu.VMEM((2, 2, PLANE, *piece), bf16),
        pltpu.VMEM((6, *piece), bf16),
        pltpu.VMEM((8, 256), jnp.int32),
        pltpu.VMEM((4, 8, 256), jnp.int32),
        pltpu.SMEM((4, 8, 256), jnp.int32),
        pltpu.VMEM((1024, WIDTH), bf16), pltpu.VMEM((512, WIDTH), bf16),
        pltpu.VMEM((6, *rows), f32),
        pltpu.VMEM((6, *rows), f32),
        pltpu.VMEM((6, *rows), f32),
        pltpu.VMEM((6, *rows), bf16),
        pltpu.VMEM((384, 1024), bf16), pltpu.VMEM((384, 512), bf16),
        pltpu.VMEM((384, WIDTH), f32),
        pltpu.VMEM((192, WIDTH), bf16),
        pltpu.VMEM((192, WIDTH), bf16),
        dma((2, 2, 4)), dma((2, 3)), dma((2, 2)), dma((2, 8)), dma((2, 2, 8)), dma((2, 2, 8)), dma((2, 2)),
        dma((6, 2, 3)), dma((CHUNKS, 2)),
        dma((2, 8)), dma((2, 8)), dma((6,)), dma((4,)), dma((2, 2, 8)), dma((2, 2, 8)), dma((2, 2)), dma((2, 2)),
        dma((2, 3)), dma((CHUNKS, 2)), dma,
    ]
    any_space = pl.BlockSpec(memory_space=pl.ANY)
    vmem = pl.BlockSpec(memory_space=pltpu.VMEM)
    by_block = [a.reshape(PER_GROUP, BLK, GROUP) for a in (queries, keys, values)]
    return pl.pallas_call(
        kernel,
        out_shape=jax.ShapeDtypeStruct((192, WIDTH), bf16),
        in_specs=[any_space, any_space, any_space, vmem, any_space],
        out_specs=vmem,
        scratch_shapes=scratch,
        compiler_params=pltpu.CompilerParams(
            collective_id=0, has_side_effects=True, vmem_limit_bytes=60 * 2**20
        ),
        name="attention",
    )(*by_block, block_mask, out_weight)


def solution(mesh):
    in_specs = (
        P("frame", "head"),
        P("frame", "head"),
        P("frame", "head"),
        P("frame", None),
        P("head", None),
    )
    out_specs = P(("frame", "head"), None)
    return jax.shard_map(
        per_device, mesh=mesh, in_specs=in_specs, out_specs=out_specs, check_vma=False
    )
```

time: 145 us -> 118 us (0.81)
  the two profiles are of different devices: /device:TPU:39 before, /device:TPU:49 now
where the time goes in v1:
time: 118 us; the launch traced here: 116 us
  Pallas kernels  114 us (97%)
  local copies, waits for them, and re-layouts  2.36 us (2%)
    pallas_call x1, Pallas kernels, per_device(): pl.pallas_call(kernel, out_shape=jax.ShapeDtypeStruct((192, WIDTH), bf16)...  114 us
    unnamed x1, local copies, waits for them, and re-layouts  2.36 us

profile of v1, /device:TPU:49, one launch (start us, length us, event | category | flops | bytes accessed | tf_op | source)
XLA Modules:
  0.0 116.2 jit_solution(9467008389807374319)
XLA Ops:
  0.0 113.9 %attention.1 = bf16[192,3072]{1,0:T(8,128)(2,1)} custom-call(bf16[6,128,768]{2,1,0:T(8,128)(2,1)} %bitcast.3, bf16[6,128,768]{2,1,0:T(8,128)(2,1)} %bitcast.4, bf16[6,128,768]{2,1,0:T(8,128)(2,1)} %bitcast.5, s32[6,192]{1,0:T(8,128)} %mask_ref.1, bf16[768,3072]{1,0:T(8,128)(2,1)} %w_hbm.1), custom_call_target="tpu_custom_call" | custom-call | tf_op jit(solution)/shard_map/attention/pallas_call | solution.py:519
  113.9 2.4 %copy.7 = bf16[192,3072]{1,0:T(8,128)(2,1)} copy(bf16[192,3072]{1,0:T(8,128)(2,1)} %attention.1) | data formatting | bytes 2359296

commit v2 on v1

--- a/solution.py
+++ b/solution.py
@@ -45,10 +45,10 @@
     q_hbm, k_hbm, v_hbm, mask_ref, w_hbm, out_ref,
     plane_a, plane_c, z_a, z_c, qbuf, blocks_ref, idx_v, idx_s, w_a, w_c, acc, top_s, sum_s, obuf, att_a, att_c,
     sums, sbuf, rbuf,
-    kv_ss, q_ss, i_ss, pf_ss, z_ss, zf_ss, w_ss, o_ss, r_ss,
-    p_rs, pf_rs, q_rs, i_rs, z_rs, zf_rs, w_rs, w_ls, a_rs, r_rs, s_sem,
+    kv_ss, q_ss, i_ss, pf_ss, z_ss, zf_ss, w_ss, wx_ss, wg_ss, wf_ss, o_ss, oc_ss, r_ss,
+    p_rs, pf_rs, q_rs, i_rs, z_rs, zf_rs, w_rs, w_ls, wx_rs, wg_rs, wf_rs, a_rs, ac_rs, r_rs, s_sem,
 ):
-    plane, zbuf, att, wbuf = (plane_a, plane_c), (z_a, z_c), (att_a, att_c), (w_a, w_c)
+    plane, zbuf, wbuf = (plane_a, plane_c), (z_a, z_c), (w_a, w_c)
     f = lax.axis_index("frame")
     h = lax.axis_index("head")
     z, yh, x = f // 8, lax.rem(f // 4, 2), lax.rem(f, 4)
@@ -94,7 +94,7 @@
         pl.semaphore_signal(barrier, inc=1, device_id=target, device_id_type=MESH)
 
     def greet_plane(i, carry):
-        target = device(z, i // 2, yl, lax.rem(i, 2))
+        target = device(z, i // 4, lax.rem(i // 2, 2), lax.rem(i, 2))
 
         @pl.when(jnp.logical_not(is_me(target)))
         def _():
@@ -102,69 +102,83 @@
 
         return carry
 
-    lax.fori_loop(0, 2 * PLANE, greet_plane, 0)
+    lax.fori_loop(0, 4 * PLANE, greet_plane, 0)
     partner = [device(z, g_me, 1 - yl, c), device(z, (1 - yh) * 4 + x, 1 - yl, c)]
-    for target in partner:
-        greet(target)
     low, high = device(z - 1, g_me, yl, c), device(z + 1, g_me, yl, c)
-
-    @pl.when(has_low)
-    def _():
-        greet(low)
-
-    @pl.when(has_high)
-    def _():
-        greet(high)
-
+    for n in range(1, 4):
+        greet(device(lax.rem(z + n, 4), g_me, yl, c))
     blocks_ref[...] = jnp.zeros_like(blocks_ref)
     blocks_ref[:PER_GROUP, : mask_ref.shape[1]] = mask_ref[...]
     blocks_ref[...] = live_blocks(blocks_ref[...])
-    pl.semaphore_wait(barrier, 17 + has_low.astype(jnp.int32) + has_high.astype(jnp.int32))
+    pl.semaphore_wait(barrier, 4 * PLANE - 1 + 3)
 
     e_me = x + yh * (3 - 2 * x)
 
-    def idx_copies():
-        for i in range(2):
-            for j in range(2):
-                yield (blocks_ref, idx_v.at[e_me], i_ss.at[i, j], i_rs.at[e_me],
-                       device(z, j * 4 + 2 * c + i, yl, yh))
-
     def kv_copies(hs):
-        for n, (j, to) in (((0, (0, 0)), (1, (1, 1))), ((2, (2, 0)), (3, (2, 1))))[hs]:
-            for i in range(2):
-                for t, src in enumerate((k_hbm, v_hbm)):
-                    yield (src.at[:, :, pl.ds((3 * i + j) * HEAD_DIM, HEAD_DIM)], plane[hs].at[t, g_me],
-                           kv_ss.at[t, i, n], p_rs.at[hs, g_me], device(z, to * 4 + 2 * c + i, yl, t))
+        for n, (row, m) in enumerate(((0, 0), (0, 1), (1, 0), (1, 1))):
+            to, i = lax.bitwise_xor(yh, row), lax.bitwise_xor(lax.rem(x, 2), m)
+            at = pl.multiple_of((3 * i + (2 if hs else to)) * HEAD_DIM, HEAD_DIM)
+            for t, src in enumerate((k_hbm, v_hbm)):
+                yield (src.at[:, :, pl.ds(at, HEAD_DIM)], plane[hs].at[t, g_me],
+                       kv_ss.at[t, hs, n], p_rs.at[hs, g_me], device(z, to * 4 + 2 * c + i, yl, t))
 
     def q_copies(hs):
         for i in range(2):
             for j in ((0, 1), (2,))[hs]:
-                to, slot = (j, e_me) if j < 2 else (e_me // 2, 4 + lax.rem(e_me, 2))
+                to, slot, core = (j, e_me, yh) if j < 2 else (yh, 4 + lax.rem(e_me, 2), e_me // 2)
+                target = device(z, to * 4 + 2 * c + i, yl, core)
+                yield blocks_ref, idx_v.at[slot], i_ss.at[i, j], i_rs.at[slot], target
                 yield (q_hbm.at[:, :, pl.ds((3 * i + j) * HEAD_DIM, HEAD_DIM)], qbuf.at[slot],
-                       q_ss.at[i, j], q_rs.at[slot], device(z, to * 4 + 2 * c + i, yl, yh))
-
-    dealt = (lambda: kv_copies(0), idx_copies, lambda: q_copies(0), lambda: kv_copies(1), lambda: q_copies(1))
+                       q_ss.at[i, j], q_rs.at[slot], target)
+
+    dealt = (lambda: kv_copies(0), lambda: q_copies(0), lambda: kv_copies(1), lambda: q_copies(1))
     for copies in dealt:
         for args in copies():
             send_or_copy(*args)
+
+    def w_row(core, i, hs):
+        return pl.multiple_of(yl * 512 + (2 * core + i) * 128 if hs else (2 * core + i) * 256, 128)
 
     def w_copies():
         for i in range(2):
             for hs, size in enumerate((256, 128)):
                 yield (w_hbm.at[pl.ds(384 * i + 256 * hs, size), :],
-                       wbuf[hs].at[pl.ds(pl.multiple_of((2 * c + i) * size, size), size), :], i, hs)
+                       wbuf[hs].at[pl.ds(w_row(c, i, hs), size), :], i, hs)
 
     for src, dst, i, hs in w_copies():
         pltpu.make_async_copy(src, dst, w_ls.at[i, hs]).start()
 
+    def far_rows(core, part, size):
+        return pl.ds(pl.multiple_of((1 - yl) * 512 + core * 256 + 64 * part, 64), size)
+
+    quarter = jnp.where(c == 0, x, z)
+
+    def w_across(k):
+        row = pl.multiple_of((quarter // 2) * 384 + 256 + 64 * lax.rem(quarter, 2) + 32 * k, 32)
+        there = pl.ds(pl.multiple_of(yl * 512 + c * 256 + 64 * quarter + 32 * k, 32), 32)
+        return remote(w_hbm.at[pl.ds(row, 32), :], w_c.at[there, :], wx_ss.at[k], wx_rs.at[k], partner[k])
+
+    def w_round(n):
+        here = w_c.at[far_rows(c, quarter, 64), :]
+        x_to = jnp.where(c == 0, lax.rem(x + n + 1, 4), x)
+        z_to = jnp.where(c == 0, z, lax.rem(z + n + 1, 4))
+        return remote(here, here, wg_ss.at[n], wg_rs.at[n], device(z_to, yh * 4 + x_to, yl, c))
+
+    def w_swap():
+        here = w_c.at[far_rows(c, 0, 256), :]
+        return remote(here, here, wf_ss, wf_rs, other_core)
+
+    for k in range(2):
+        w_across(k).start()
+
     def frame_of(step):
         return lax.bitwise_xor(step, g_me)
 
     def to_high(hs, g):
-        return (g // 2 != 1 - yh) if hs else (g >= 0)
+        return ((yh == 0) | (g // 4 == 1)) if hs else (g >= 0)
 
     def to_low(hs, g):
-        return (g // 2 != 2 + yh) if hs else (g >= 0)
+        return ((yh == 1) | (g // 4 == 0)) if hs else (g >= 0)
 
     def z_copy(way, hs, g):
         return remote(plane[hs].at[c, g], zbuf[hs].at[way, c, g], z_ss.at[way, hs, g], z_rs.at[way, hs, g],
@@ -231,8 +245,10 @@
 
         lax.fori_loop(0, PLANE, one, 0)
 
-    def frame_at(e):
-        return e + c * (7 - 2 * e)
+    side_of = (c, yh)
+
+    def frame_at(e, side):
+        return e + side * (7 - 2 * e)
 
     def scores_of(q, keys):
         return lax.dot_general(q, keys, (((1,), (1,)), ((), ())), preferred_element_type=jnp.float32)
@@ -240,19 +256,23 @@
     def rows_at(qb):
         return pl.ds(pl.multiple_of(qb * BLK, BLK), BLK)
 
-    def block(e, qb, distance, way, j=0):
-        group = z * PLANE + frame_at(e) + (2 * way - 1) * distance
-        group = jnp.clip(group, 0, 4 * PLANE - 1)
-        return idx_s[e, qb, group * PER_GROUP + j]
+    def block(u, qb, g, way, distance, j=0):
+        group = jnp.clip(z * PLANE + g + (2 * way - 1) * distance, 0, 4 * PLANE - 1)
+        return idx_s[u, qb, group * PER_GROUP + j]
 
     def plane_part(u, e, hs, out1, out2, qb):
-        g = frame_at(e)
-        near = [(frame_at(e + 1), block(e, qb, 1, 1 - c, j)) for j in range(3)]
-        near += [(frame_at(e + 2), block(e, qb, 2, 1 - c)), (frame_at(e + 4), block(e, qb, 4, 1 - c))]
+        side = side_of[hs]
+        g = frame_at(e, side)
+
+        def near_block(by, j=0):
+            way = 1 - side if by > 0 else side
+            return frame_at(e + by, side), block(u, qb, g, way, abs(by), j)
+
+        near = [near_block(1, j) for j in range(3)] + [near_block(2), near_block(4)]
         if out1:
-            near += [(frame_at(e - 1), block(e, qb, 1, c, j)) for j in range(3)]
+            near += [near_block(-1, j) for j in range(3)]
         if out2:
-            near += [(frame_at(e - 2), block(e, qb, 2, c))]
+            near += [near_block(-2)]
         q = qbuf[u, qb]
 
         def taken(t):
@@ -270,12 +290,17 @@
         sum_s[u, rows_at(qb), :] = jnp.broadcast_to(total, (BLK, HEAD_DIM))
 
     def z_part(u, e, hs, out1, out2, qb):
-        g = frame_at(e)
-        far = [(0, g, block(e, qb, 8, 0)), (1, g, block(e, qb, 8, 1)), (c, frame_at(e + 4), block(e, qb, 4, c))]
+        side = side_of[hs]
+        g = frame_at(e, side)
+
+        def far_block(distance, j=0):
+            return side, frame_at(e + PLANE - distance, side), block(u, qb, g, side, distance, j)
+
+        far = [(way, g, block(u, qb, g, way, 8)) for way in range(2)] + [far_block(4)]
         if not out2:
-            far += [(c, frame_at(e + 6), block(e, qb, 2, c))]
+            far += [far_block(2)]
         if not out1:
-            far += [(c, frame_at(e + 7), block(e, qb, 1, c, j)) for j in range(3)]
+            far += [far_block(1, j) for j in range(3)]
         q = qbuf[u, qb]
         keys, vals, valid = [], [], []
         for way, gg, b in far:
@@ -306,23 +331,24 @@
 
         lax.fori_loop(0, last, one, 0, unroll=unroll)
 
-    def o_copies(u, e, hs, ks):
-        head = x if hs else 2 * x + yh
-        cols = pl.ds(pl.multiple_of(head * HEAD_DIM, HEAD_DIM), HEAD_DIM)
-        x_to = e + c * (3 - 2 * e)
+    def own_o_copies(u):
+        cols = pl.ds(pl.multiple_of((2 * x + yh) * HEAD_DIM, HEAD_DIM), HEAD_DIM)
+        x_to = u + c * (3 - 2 * u)
         here, across = c * 4 + x_to, (1 - c) * 4 + x_to
         for t in range(2):
             mine, theirs = (2 * yl + t) * 192, (2 * (1 - yl) + t) * 192
             parts = ((mine, 192, 192, here), (theirs, 96, 0, here), (theirs + 96, 96, 96, across))
-            for k in ks:
-                row, size, at, to = parts[k]
-                yield (obuf.at[u, pl.ds(pl.multiple_of(row, 96), size), :], att[hs].at[pl.ds(at, size), cols],
-                       o_ss.at[u, t, k], a_rs.at[hs, k], device(z, to, yl, t))
-
-    def att_arrived(hs, ks):
-        for k in ks:
-            row, size = ((192, 192), (0, 96), (96, 96))[k]
-            arrived(att[hs].at[pl.ds(row, size)], a_rs.at[hs, k])
+            for k, (row, size, at, to) in enumerate(parts):
+                yield (obuf.at[u, pl.ds(pl.multiple_of(row, 96), size), :], att_a.at[pl.ds(at, size), cols],
+                       o_ss.at[u, t, k], a_rs.at[k], device(z, to, yl, t))
+
+    def shared_o_copies(u, e):
+        cols = pl.ds(pl.multiple_of(yl * 512 + x * HEAD_DIM, HEAD_DIM), HEAD_DIM)
+        to = yh * 4 + e + yh * (3 - 2 * e)
+        for yl_to in range(2):
+            for t in range(2):
+                yield (obuf.at[u, pl.ds((2 * yl_to + t) * 192, 192), :], att_c.at[:, cols],
+                       oc_ss.at[u - 4, 2 * yl_to + t], ac_rs, device(z, to, yl_to, t))
 
     own_kinds = (
         (1, lambda n: (0, 0), False, False),
@@ -330,22 +356,25 @@
         (2, lambda n: (2 + n, 2 + n), True, True),
     )
     shared_kinds = (
-        (1 - yh, lambda n: (4, 0), False, False),
-        (1 - yh, lambda n: (5, 1), True, False),
-        (2 * yh, lambda n: (4 + n, 2 + n), True, True),
+        (1 - c, lambda n: (4, 0), False, False),
+        (1 - c, lambda n: (5, 1), True, False),
+        (2 * c, lambda n: (4 + n, 2 + n), True, True),
     )
+
+    def units_ready(first, last):
+        for u in range(first, last):
+            arrived(idx_v.at[u], i_rs.at[u])
+        load = pltpu.make_async_copy(idx_v.at[pl.ds(first, last - first)], idx_s.at[pl.ds(first, last - first)], s_sem)
+        load.start()
+        load.wait()
+        for u in range(first, last):
+            arrived(qbuf.at[u], q_rs.at[u])
 
     spread(0, 0, PLANE)
     for src, dst, i, hs in w_copies():
         remote(src, dst, w_ss.at[i, hs], w_rs.at[i, hs], other_core).start()
-    for e in range(4):
-        arrived(idx_v.at[e], i_rs.at[e])
-    load_idx = pltpu.make_async_copy(idx_v, idx_s, s_sem)
-    load_idx.start()
     other_plane(0)
-    load_idx.wait()
-    for u in range(4):
-        arrived(qbuf.at[u], q_rs.at[u])
+    units_ready(0, 4)
     for count, unit, out1, out2 in own_kinds:
 
         def own_plane(n, carry, unit=unit, out1=out1, out2=out2):
@@ -356,21 +385,24 @@
             return carry
 
         lax.fori_loop(0, count, own_plane, 0)
+    for k in range(2):
+        w_across(k).wait_recv()
+    for n in range(3):
+        w_round(n).start()
     other_z(0)
     for count, unit, out1, out2 in own_kinds:
 
         def own_far(n, carry, unit=unit, out1=out1, out2=out2):
             u, e = unit(n)
             query_blocks(0, PER_GROUP, 6, z_part, u, e, 0, out1, out2)
-            for args in o_copies(u, e, 0, range(3)):
+            for args in own_o_copies(u):
                 send_or_copy(*args)
             return carry
 
         lax.fori_loop(0, count, own_far, 0)
     pass_on(1, 0, 1)
     other_plane(1)
-    for u in range(4, 6):
-        arrived(qbuf.at[u], q_rs.at[u])
+    units_ready(4, 6)
     for count, unit, out1, out2 in shared_kinds:
 
         def shared_plane(n, carry, unit=unit, out1=out1, out2=out2):
@@ -385,14 +417,23 @@
         pltpu.make_async_copy(src, dst, w_ls.at[i, hs]).wait()
     for i in range(2):
         for hs, size in enumerate((256, 128)):
-            arrived(wbuf[hs].at[pl.ds(pl.multiple_of((2 * (1 - c) + i) * size, size), size), :], w_rs.at[i, hs])
-    att_arrived(0, range(3))
+            arrived(wbuf[hs].at[pl.ds(w_row(1 - c, i, hs), size), :], w_rs.at[i, hs])
+    for k, (row, size) in enumerate(((192, 192), (0, 96), (96, 96))):
+        arrived(att_a.at[pl.ds(row, size)], a_rs.at[k])
 
     def cols_at(n):
         return pl.ds(pl.multiple_of(n * CHUNK, CHUNK), CHUNK)
 
+    def r_copy(n, k):
+        rows = pl.ds(96 * k, 96)
+        return remote(sbuf.at[rows, cols_at(n)], rbuf.at[rows, cols_at(n)], r_ss.at[n, k], r_rs.at[n, k], partner[k])
+
     def project_own(n, carry):
-        sums[:, cols_at(n)] = jnp.dot(att_a[...], w_a[:, cols_at(n)], preferred_element_type=jnp.float32)
+        r = jnp.dot(att_a[...], w_a[:, cols_at(n)], preferred_element_type=jnp.float32)
+        sbuf[:, cols_at(n)] = r[:192].astype(jnp.bfloat16)
+        sums[:, cols_at(n)] = r[192:]
+        for k in range(2):
+            r_copy(n, k).start()
         return carry
 
     def project_and_pass(n, carry):
@@ -402,46 +443,31 @@
 
     lax.fori_loop(0, 5, project_and_pass, 0)
     lax.fori_loop(5, CHUNKS, project_own, 0)
+    for n in range(3):
+        arrived(w_c.at[far_rows(c, lax.rem(quarter + 3 - n, 4), 64), :], wg_rs.at[n])
+    w_swap().start()
     other_z(1)
-    for ks, first in (((1, 2), 3 * (1 - yl)), ((0,), 3 * yl)):
-        for count, unit, out1, out2 in shared_kinds:
-
-            def shared_far(n, carry, unit=unit, out1=out1, out2=out2):
-                u, e = unit(n)
-                query_blocks(first, 3, 3, z_part, u, e, 1, out1, out2)
-                for args in o_copies(u, e, 1, ks):
-                    send_or_copy(*args)
-                return carry
-
-            lax.fori_loop(0, count, shared_far, 0)
-
-    def r_copy(n, k):
-        rows = pl.ds(96 * k, 96)
-        return remote(sbuf.at[rows, cols_at(n)], rbuf.at[rows, cols_at(n)], r_ss.at[n, k], r_rs.at[n, k], partner[k])
-
-    def project_theirs(n, carry):
-        r = jnp.dot(att_c[:192], w_c[:, cols_at(n)], preferred_element_type=jnp.float32)
-        sbuf[:, cols_at(n)] = (r + sums[:192, cols_at(n)]).astype(jnp.bfloat16)
-        for k in range(2):
-            r_copy(n, k).start()
-        return carry
-
-    def project_mine(n, carry):
-        r = jnp.dot(att_c[192:], w_c[:, cols_at(n)], preferred_element_type=jnp.float32)
-        sums[192:, cols_at(n)] = r + sums[192:, cols_at(n)]
-        return carry
+    for count, unit, out1, out2 in shared_kinds:
+
+        def shared_far(n, carry, unit=unit, out1=out1, out2=out2):
+            u, e = unit(n)
+            query_blocks(0, PER_GROUP, 6, z_part, u, e, 1, out1, out2)
+            for args in shared_o_copies(u, e):
+                send_or_copy(*args)
+            return carry
+
+        lax.fori_loop(0, count, shared_far, 0)
 
     def finish(n, carry):
         for k in range(2):
             r_copy(n, k).wait()
-        total = sums[192:, cols_at(n)] + rbuf[:, cols_at(n)].astype(jnp.float32)
+        total = sums[:, cols_at(n)] + rbuf[:, cols_at(n)].astype(jnp.float32)
+        total = total + jnp.dot(att_c[...], w_c[:, cols_at(n)], preferred_element_type=jnp.float32)
         out_ref[:, cols_at(n)] = total.astype(jnp.bfloat16)
         return carry
 
-    att_arrived(1, (1, 2))
-    lax.fori_loop(0, CHUNKS, project_theirs, 0)
-    att_arrived(1, (0,))
-    lax.fori_loop(0, CHUNKS, project_mine, 0)
+    arrived(w_c.at[far_rows(1 - c, 0, 256), :], wf_rs)
+    arrived(att_c, ac_rs)
     lax.fori_loop(0, CHUNKS, finish, 0)
 
     for copies in dealt:
@@ -472,16 +498,20 @@
 
     lax.fori_loop(0, PLANE, done, 0)
 
-    def o_done(u, e, hs):
-        for args in o_copies(u, e, hs, range(3)):
+    for k in range(2):
+        w_across(k).wait_send()
+    for n in range(3):
+        w_round(n).wait_send()
+    w_swap().wait_send()
+
+    def own_done(u, carry):
+        for args in own_o_copies(u):
             sent(*args)
-
-    def own_done(n, carry):
-        o_done(n, n, 0)
         return carry
 
     def shared_done(n, carry):
-        o_done(4 + n, 2 * yh + n, 1)
+        for args in shared_o_copies(4 + n, 2 * c + n):
+            sent(*args)
         return carry
 
     lax.fori_loop(0, 4, own_done, 0)
@@ -497,21 +527,21 @@
         pltpu.VMEM((2, 2, PLANE, *piece), bf16), pltpu.VMEM((2, 2, PLANE, *piece), bf16),
         pltpu.VMEM((6, *piece), bf16),
         pltpu.VMEM((8, 256), jnp.int32),
-        pltpu.VMEM((4, 8, 256), jnp.int32),
-        pltpu.SMEM((4, 8, 256), jnp.int32),
-        pltpu.VMEM((1024, WIDTH), bf16), pltpu.VMEM((512, WIDTH), bf16),
+        pltpu.VMEM((6, 8, 256), jnp.int32),
+        pltpu.SMEM((6, 8, 256), jnp.int32),
+        pltpu.VMEM((1024, WIDTH), bf16), pltpu.VMEM((1024, WIDTH), bf16),
         pltpu.VMEM((6, *rows), f32),
         pltpu.VMEM((6, *rows), f32),
         pltpu.VMEM((6, *rows), f32),
         pltpu.VMEM((6, *rows), bf16),
-        pltpu.VMEM((384, 1024), bf16), pltpu.VMEM((384, 512), bf16),
-        pltpu.VMEM((384, WIDTH), f32),
+        pltpu.VMEM((384, 1024), bf16), pltpu.VMEM((192, 1024), bf16),
+        pltpu.VMEM((192, WIDTH), f32),
         pltpu.VMEM((192, WIDTH), bf16),
         pltpu.VMEM((192, WIDTH), bf16),
-        dma((2, 2, 4)), dma((2, 3)), dma((2, 2)), dma((2, 8)), dma((2, 2, 8)), dma((2, 2, 8)), dma((2, 2)),
-        dma((6, 2, 3)), dma((CHUNKS, 2)),
-        dma((2, 8)), dma((2, 8)), dma((6,)), dma((4,)), dma((2, 2, 8)), dma((2, 2, 8)), dma((2, 2)), dma((2, 2)),
-        dma((2, 3)), dma((CHUNKS, 2)), dma,
+        dma((2, 2, 4)), dma((2, 3)), dma((2, 3)), dma((2, 8)), dma((2, 2, 8)), dma((2, 2, 8)), dma((2, 2)),
+        dma((2,)), dma((3,)), dma, dma((4, 2, 3)), dma((2, 4)), dma((CHUNKS, 2)),
+        dma((2, 8)), dma((2, 8)), dma((6,)), dma((6,)), dma((2, 2, 8)), dma((2, 2, 8)), dma((2, 2)), dma((2, 2)),
+        dma((2,)), dma((3,)), dma, dma((3,)), dma, dma((CHUNKS, 2)), dma,
     ]
     any_space = pl.BlockSpec(memory_space=pl.ANY)
     vmem = pl.BlockSpec(memory_space=pltpu.VMEM)

time: 118 us -> 110 us (0.932)
  the two profiles are of different devices: /device:TPU:49 before, /device:TPU:1 now
where the time goes in v2:
time: 110 us
  Pallas kernels  107 us (97%)
  local copies, waits for them, and re-layouts  2.36 us (2%)
    pallas_call x1, Pallas kernels, per_device(): pl.pallas_call(kernel, out_shape=jax.ShapeDtypeStruct((192, WIDTH), bf16)...  107 us
    unnamed x1, local copies, waits for them, and re-layouts  2.36 us

profile of v2, /device:TPU:1, one launch (start us, length us, event | category | flops | bytes accessed | tf_op | source)
XLA Modules:
  0.0 109.5 jit_solution(13112066843470026415)
XLA Ops:
  0.0 107.1 %attention.1 = bf16[192,3072]{1,0:T(8,128)(2,1)} custom-call(bf16[6,128,768]{2,1,0:T(8,128)(2,1)} %bitcast.3, bf16[6,128,768]{2,1,0:T(8,128)(2,1)} %bitcast.4, bf16[6,128,768]{2,1,0:T(8,128)(2,1)} %bitcast.5, s32[6,192]{1,0:T(8,128)} %mask_ref.1, bf16[768,3072]{1,0:T(8,128)(2,1)} %w_hbm.1), custom_call_target="tpu_custom_call" | custom-call | tf_op jit(solution)/shard_map/attention/pallas_call | solution.py:549
  107.1 2.4 %copy.7 = bf16[192,3072]{1,0:T(8,128)(2,1)} copy(bf16[192,3072]{1,0:T(8,128)(2,1)} %attention.1) | data formatting | bytes 2359296

commit v3 on v2

--- a/solution.py
+++ b/solution.py
@@ -93,24 +93,23 @@
     def greet(target):
         pl.semaphore_signal(barrier, inc=1, device_id=target, device_id_type=MESH)
 
-    def greet_plane(i, carry):
-        target = device(z, i // 4, lax.rem(i // 2, 2), lax.rem(i, 2))
-
-        @pl.when(jnp.logical_not(is_me(target)))
-        def _():
-            greet(target)
-
-        return carry
-
-    lax.fori_loop(0, 4 * PLANE, greet_plane, 0)
+    dealer = x // 2
+
+    def greet_plane(g, carry):
+        greet(device(z, g, yl, jnp.where(g == g_me, 1 - c, dealer)))
+        return carry
+
+    lax.fori_loop(0, PLANE, greet_plane, 0)
     partner = [device(z, g_me, 1 - yl, c), device(z, (1 - yh) * 4 + x, 1 - yl, c)]
+    for target in partner:
+        greet(target)
     low, high = device(z - 1, g_me, yl, c), device(z + 1, g_me, yl, c)
     for n in range(1, 4):
         greet(device(lax.rem(z + n, 4), g_me, yl, c))
     blocks_ref[...] = jnp.zeros_like(blocks_ref)
     blocks_ref[:PER_GROUP, : mask_ref.shape[1]] = mask_ref[...]
     blocks_ref[...] = live_blocks(blocks_ref[...])
-    pl.semaphore_wait(barrier, 4 * PLANE - 1 + 3)
+    pl.semaphore_wait(barrier, jnp.where(dealer == c, 7, 9) + 2 + 3)
 
     e_me = x + yh * (3 - 2 * x)
 
@@ -380,15 +379,11 @@
         def own_plane(n, carry, unit=unit, out1=out1, out2=out2):
             u, e = unit(n)
             query_blocks(0, PER_GROUP, 3, plane_part, u, e, 0, out1, out2)
-            spread(1, 2 * u, 2 * u + 2)
+            spread(1, u, u + 1)
             pass_on(0, 2 * u, 2 * u + 2)
             return carry
 
         lax.fori_loop(0, count, own_plane, 0)
-    for k in range(2):
-        w_across(k).wait_recv()
-    for n in range(3):
-        w_round(n).start()
     other_z(0)
     for count, unit, out1, out2 in own_kinds:
 
@@ -400,6 +395,7 @@
             return carry
 
         lax.fori_loop(0, count, own_far, 0)
+    spread(1, 4, PLANE)
     pass_on(1, 0, 1)
     other_plane(1)
     units_ready(4, 6)
@@ -441,6 +437,10 @@
         pass_on(1, n + 3, n + 4)
         return carry
 
+    for k in range(2):
+        w_across(k).wait_recv()
+    for n in range(3):
+        w_round(n).start()
     lax.fori_loop(0, 5, project_and_pass, 0)
     lax.fori_loop(5, CHUNKS, project_own, 0)
     for n in range(3):
@@ -466,10 +466,6 @@
         out_ref[:, cols_at(n)] = total.astype(jnp.bfloat16)
         return carry
 
-    arrived(w_c.at[far_rows(1 - c, 0, 256), :], wf_rs)
-    arrived(att_c, ac_rs)
-    lax.fori_loop(0, CHUNKS, finish, 0)
-
     for copies in dealt:
         for args in copies():
             sent(*args)
@@ -509,12 +505,16 @@
             sent(*args)
         return carry
 
+    lax.fori_loop(0, 4, own_done, 0)
+    arrived(w_c.at[far_rows(1 - c, 0, 256), :], wf_rs)
+    arrived(att_c, ac_rs)
+    lax.fori_loop(0, CHUNKS, finish, 0)
+
     def shared_done(n, carry):
         for args in shared_o_copies(4 + n, 2 * c + n):
             sent(*args)
         return carry
 
-    lax.fori_loop(0, 4, own_done, 0)
     lax.fori_loop(0, 2, shared_done, 0)
 
 
@@ -548,7 +548,7 @@
     by_block = [a.reshape(PER_GROUP, BLK, GROUP) for a in (queries, keys, values)]
     return pl.pallas_call(
         kernel,
-        out_shape=jax.ShapeDtypeStruct((192, WIDTH), bf16),
+        out_shape=pltpu.VMEM((192, WIDTH), bf16),
         in_specs=[any_space, any_space, any_space, vmem, any_space],
         out_specs=vmem,
         scratch_shapes=scratch,

time: 110 us -> 108 us (0.982)
  the two profiles are of different devices: /device:TPU:1 before, /device:TPU:49 now
where the time goes in v3:
time: 108 us; the launch traced here: 107 us
  Pallas kernels  106 us (98%)
    pallas_call x1, Pallas kernels, per_device(): pl.pallas_call(kernel, out_shape=pltpu.VMEM((192, WIDTH), bf16), in_specs...  106 us

profile of v3, /device:TPU:49, one launch (start us, length us, event | category | flops | bytes accessed | tf_op | source)
XLA Modules:
  0.0 107.4 jit_solution(3941622980550660822)
XLA Ops:
  0.0 106.4 %attention.1 = bf16[192,3072]{1,0:T(8,128)(2,1)S(1)} custom-call(bf16[6,128,768]{2,1,0:T(8,128)(2,1)} %bitcast.3, bf16[6,128,768]{2,1,0:T(8,128)(2,1)} %bitcast.4, bf16[6,128,768]{2,1,0:T(8,128)(2,1)} %bitcast.5, s32[6,192]{1,0:T(8,128)} %mask_ref.1, bf16[768,3072]{1,0:T(8,128)(2,1)} %w_hbm.1), custom_call_target="tpu_custom_call" | custom-call | tf_op jit(solution)/shard_map/attention/pallas_call | solution.py:549
  106.4 1.0 copy.7

commit v4 on v3

--- a/solution.py
+++ b/solution.py
@@ -42,8 +42,8 @@
 
 
 def kernel(
-    q_hbm, k_hbm, v_hbm, mask_ref, w_hbm, out_ref,
-    plane_a, plane_c, z_a, z_c, qbuf, blocks_ref, idx_v, idx_s, w_a, w_c, acc, top_s, sum_s, obuf, att_a, att_c,
+    q_hbm, k_hbm, v_hbm, mask_hbm, w_hbm, out_ref,
+    mask_ref, plane_a, plane_c, z_a, z_c, qbuf, blocks_ref, idx_v, idx_s, w_a, w_c, acc, top_s, sum_s, obuf, att_a, att_c,
     sums, sbuf, rbuf,
     kv_ss, q_ss, i_ss, pf_ss, z_ss, zf_ss, w_ss, wx_ss, wg_ss, wf_ss, o_ss, oc_ss, r_ss,
     p_rs, pf_rs, q_rs, i_rs, z_rs, zf_rs, w_rs, w_ls, wx_rs, wg_rs, wf_rs, a_rs, ac_rs, r_rs, s_sem,
@@ -88,6 +88,9 @@
     def arrived(ref, sem):
         pltpu.make_async_copy(ref, ref, sem).wait()
 
+    load_mask = pltpu.make_async_copy(mask_hbm, mask_ref, s_sem)
+    load_mask.start()
+
     barrier = pltpu.get_barrier_semaphore()
 
     def greet(target):
@@ -104,12 +107,9 @@
     for target in partner:
         greet(target)
     low, high = device(z - 1, g_me, yl, c), device(z + 1, g_me, yl, c)
-    for n in range(1, 4):
+    for n in (1, 3):
         greet(device(lax.rem(z + n, 4), g_me, yl, c))
-    blocks_ref[...] = jnp.zeros_like(blocks_ref)
-    blocks_ref[:PER_GROUP, : mask_ref.shape[1]] = mask_ref[...]
-    blocks_ref[...] = live_blocks(blocks_ref[...])
-    pl.semaphore_wait(barrier, jnp.where(dealer == c, 7, 9) + 2 + 3)
+    pl.semaphore_wait(barrier, jnp.where(dealer == c, 7, 9) + 2 + 2)
 
     e_me = x + yh * (3 - 2 * x)
 
@@ -131,7 +131,13 @@
                        q_ss.at[i, j], q_rs.at[slot], target)
 
     dealt = (lambda: kv_copies(0), lambda: q_copies(0), lambda: kv_copies(1), lambda: q_copies(1))
-    for copies in dealt:
+    for args in dealt[0]():
+        send_or_copy(*args)
+    load_mask.wait()
+    blocks_ref[...] = jnp.zeros_like(blocks_ref)
+    blocks_ref[:PER_GROUP, : mask_ref.shape[1]] = mask_ref[...]
+    blocks_ref[...] = live_blocks(blocks_ref[...])
+    for copies in dealt[1:]:
         for args in copies():
             send_or_copy(*args)
 
@@ -150,18 +156,15 @@
     def far_rows(core, part, size):
         return pl.ds(pl.multiple_of((1 - yl) * 512 + core * 256 + 64 * part, 64), size)
 
-    quarter = jnp.where(c == 0, x, z)
-
     def w_across(k):
-        row = pl.multiple_of((quarter // 2) * 384 + 256 + 64 * lax.rem(quarter, 2) + 32 * k, 32)
-        there = pl.ds(pl.multiple_of(yl * 512 + c * 256 + 64 * quarter + 32 * k, 32), 32)
+        row = pl.multiple_of((x // 2) * 384 + 256 + 64 * lax.rem(x, 2) + 32 * k, 32)
+        there = pl.ds(pl.multiple_of(yl * 512 + c * 256 + 64 * x + 32 * k, 32), 32)
         return remote(w_hbm.at[pl.ds(row, 32), :], w_c.at[there, :], wx_ss.at[k], wx_rs.at[k], partner[k])
 
     def w_round(n):
-        here = w_c.at[far_rows(c, quarter, 64), :]
-        x_to = jnp.where(c == 0, lax.rem(x + n + 1, 4), x)
-        z_to = jnp.where(c == 0, z, lax.rem(z + n + 1, 4))
-        return remote(here, here, wg_ss.at[n], wg_rs.at[n], device(z_to, yh * 4 + x_to, yl, c))
+        here = w_c.at[far_rows(c, x, 64), :]
+        x_to = lax.rem(x + n + 1, 4)
+        return remote(here, here, wg_ss.at[n], wg_rs.at[n], device(z, yh * 4 + x_to, yl, c))
 
     def w_swap():
         here = w_c.at[far_rows(c, 0, 256), :]
@@ -443,9 +446,6 @@
         w_round(n).start()
     lax.fori_loop(0, 5, project_and_pass, 0)
     lax.fori_loop(5, CHUNKS, project_own, 0)
-    for n in range(3):
-        arrived(w_c.at[far_rows(c, lax.rem(quarter + 3 - n, 4), 64), :], wg_rs.at[n])
-    w_swap().start()
     other_z(1)
     for count, unit, out1, out2 in shared_kinds:
 
@@ -466,6 +466,9 @@
         out_ref[:, cols_at(n)] = total.astype(jnp.bfloat16)
         return carry
 
+    for n in range(3):
+        arrived(w_c.at[far_rows(c, lax.rem(x + 3 - n, 4), 64), :], wg_rs.at[n])
+    w_swap().start()
     for copies in dealt:
         for args in copies():
             sent(*args)
@@ -523,6 +526,7 @@
     bf16, f32 = jnp.bfloat16, jnp.float32
     rows, piece = (GROUP, HEAD_DIM), (PER_GROUP, BLK, HEAD_DIM)
     scratch = [
+        pltpu.VMEM(block_mask.shape, jnp.int32),
         pltpu.VMEM((2, PLANE, *piece), bf16), pltpu.VMEM((2, PLANE, *piece), bf16),
         pltpu.VMEM((2, 2, PLANE, *piece), bf16), pltpu.VMEM((2, 2, PLANE, *piece), bf16),
         pltpu.VMEM((6, *piece), bf16),
@@ -549,7 +553,7 @@
     return pl.pallas_call(
         kernel,
         out_shape=pltpu.VMEM((192, WIDTH), bf16),
-        in_specs=[any_space, any_space, any_space, vmem, any_space],
+        in_specs=[any_space] * 5,
         out_specs=vmem,
         scratch_shapes=scratch,
         compiler_params=pltpu.CompilerParams(

time: 108 us -> 105 us (0.972)
  Pallas kernels: 106 us -> 103 us
    pallas_call x1, Pallas kernels: 106 us -> 103 us  [per_device(): pl.pallas_call(kernel, out_shape=pltpu.VMEM((192, WIDTH), bf16), in_specs...]
where the time goes in v4:
time: 105 us; the launch traced here: 104 us
  Pallas kernels  103 us (98%)
    pallas_call x1, Pallas kernels, per_device(): pl.pallas_call(kernel, out_shape=pltpu.VMEM((192, WIDTH), bf16), in_specs...  103 us

profile of v4, /device:TPU:49, one launch (start us, length us, event | category | flops | bytes accessed | tf_op | source)
XLA Modules:
  0.0 104.4 jit_solution(13813035811553702120)
XLA Ops:
  0.0 103.4 %attention.1 = bf16[192,3072]{1,0:T(8,128)(2,1)S(1)} custom-call(bf16[6,128,768]{2,1,0:T(8,128)(2,1)} %bitcast.3, bf16[6,128,768]{2,1,0:T(8,128)(2,1)} %bitcast.4, bf16[6,128,768]{2,1,0:T(8,128)(2,1)} %bitcast.5, s32[6,192]{1,0:T(8,128)} %mask_hbm.1, bf16[768,3072]{1,0:T(8,128)(2,1)} %w_hbm.1), custom_call_target="tpu_custom_call" | custom-call | tf_op jit(solution)/shard_map/attention/pallas_call | solution.py:553
  103.4 1.0 copy.7

commit v5 on v4

--- a/solution.py
+++ b/solution.py
@@ -124,7 +124,7 @@
     def q_copies(hs):
         for i in range(2):
             for j in ((0, 1), (2,))[hs]:
-                to, slot, core = (j, e_me, yh) if j < 2 else (yh, 4 + lax.rem(e_me, 2), e_me // 2)
+                to, slot, core = (j, e_me, yh) if j < 2 else (yh, 4 + e_me // 2, lax.rem(e_me, 2))
                 target = device(z, to * 4 + 2 * c + i, yl, core)
                 yield blocks_ref, idx_v.at[slot], i_ss.at[i, j], i_rs.at[slot], target
                 yield (q_hbm.at[:, :, pl.ds((3 * i + j) * HEAD_DIM, HEAD_DIM)], qbuf.at[slot],
@@ -359,8 +359,8 @@
     )
     shared_kinds = (
         (1 - c, lambda n: (4, 0), False, False),
-        (1 - c, lambda n: (5, 1), True, False),
-        (2 * c, lambda n: (4 + n, 2 + n), True, True),
+        (c, lambda n: (4, 1), True, False),
+        (1, lambda n: (5, 2 + c), True, True),
     )
 
     def units_ready(first, last):
@@ -514,7 +514,7 @@
     lax.fori_loop(0, CHUNKS, finish, 0)
 
     def shared_done(n, carry):
-        for args in shared_o_copies(4 + n, 2 * c + n):
+        for args in shared_o_copies(4 + n, c + 2 * n):
             sent(*args)
         return carry
 

time: 105 us -> 105 us (level)
  no operation moved by 1% of the time
where the time goes in v5:
time: 105 us
  Pallas kernels  104 us (99%)
    pallas_call x1, Pallas kernels, per_device(): pl.pallas_call(kernel, out_shape=pltpu.VMEM((192, WIDTH), bf16), in_specs...  104 us

profile of v5, /device:TPU:49, one launch (start us, length us, event | category | flops | bytes accessed | tf_op | source)
XLA Modules:
  0.0 105.0 jit_solution(12825564306183805430)
XLA Ops:
  0.0 104.0 %attention.1 = bf16[192,3072]{1,0:T(8,128)(2,1)S(1)} custom-call(bf16[6,128,768]{2,1,0:T(8,128)(2,1)} %bitcast.3, bf16[6,128,768]{2,1,0:T(8,128)(2,1)} %bitcast.4, bf16[6,128,768]{2,1,0:T(8,128)(2,1)} %bitcast.5, s32[6,192]{1,0:T(8,128)} %mask_hbm.1, bf16[768,3072]{1,0:T(8,128)(2,1)} %w_hbm.1), custom_call_target="tpu_custom_call" | custom-call | tf_op jit(solution)/shard_map/attention/pallas_call | solution.py:553
  104.0 1.0 copy.7
